TPU v7x, 512 devices: a whole 4x4x16 slice. The times are simulated.
512 devices in a mesh: mode: 32 (over y, x, core), space: 16 (over z).
Axes of the slice: x: 4, y: 4, z: 16, core: 2. Of those that a mesh axis runs over, the one named last changes fastest.
Arguments:
- mode_field: bfloat16 [288, 128, 8, 128], P('mode', 'space'), may hold values from -6 to 6
- kl_coeff: float32 [11, 128, 8, 128], P(None, 'space'), may hold values from -4 to 4
- mode_slot: int32 [286], replicated, may hold values from 0 to 287, as said below
- trip_kl: int32 [1606], replicated, may hold values from 0 to 10, as said below
- trip_in: int32 [1606], replicated, may hold values from 0 to 285
- trip_out: int32 [1606], replicated, may hold values from 0 to 285, as said below
- trip_weight: bfloat16 [1606], replicated, may hold values from 1 to 2
Outputs:
- response: float32 [288, 128, 8, 128], P('mode', 'space')
Inputs may be any that keep to these rules, and one draw needn't show every extreme that they name: `mode_slot`: the 286 modes sit in distinct slots. `trip_kl`: each entry names a distinct triple of expansion term, input mode and output mode. `trip_out`: every mode is the output mode of some entry.
All inputs are finite; a program needn't handle non-finite values.
Results may differ from a plain program's by a relative error of at most 0.0003.
Values may be sent and summed in bfloat16 or wider, within the bound.
A program may use at most 64 MiB of HBM per device.

v0:
```python
import jax
import jax.numpy as jnp
from jax import lax
from jax.sharding import PartitionSpec as P

neighbour_steps = ((1, 0, 0), (-1, 0, 0), (0, 1, 0), (0, -1, 0), (0, 0, 1), (0, 0, -1))


def padded(block, sides, width):
    for axis, dim in sides:
        count = lax.axis_size(axis)
        forward = [(i, i + 1) for i in range(count - 1)]
        backward = [(target, source) for source, target in forward]
        low = lax.ppermute(
            lax.slice_in_dim(block, block.shape[dim] - width, None, axis=dim), axis, forward
        )
        high = lax.ppermute(lax.slice_in_dim(block, 0, width, axis=dim), axis, backward)
        block = jnp.concatenate([low, block, high], axis=dim)
    return block


def shifted(values, step_z, step_y, step_x):
    plane_count = values.shape[-3]
    row_count = values.shape[-2]
    col_count = values.shape[-1]
    return values[
        ...,
        1 + step_z : plane_count - 1 + step_z,
        1 + step_y : row_count - 1 + step_y,
        1 + step_x : col_count - 1 + step_x,
    ]


def diffusion(values, coeffs):
    centre_value = shifted(values, 0, 0, 0)
    centre_coeff = shifted(coeffs, 0, 0, 0)
    running = jnp.zeros(centre_value.shape, jnp.float32)
    for step_z, step_y, step_x in neighbour_steps:
        face_value = 0.5 * (centre_coeff + shifted(coeffs, step_z, step_y, step_x))
        running = running + face_value * (centre_value - shifted(values, step_z, step_y, step_x))
    return running


def body(mode_field, kl_coeff, mode_slot, trip_kl, trip_in, trip_out, trip_weight):
    slot_count = mode_field.shape[0]
    plane_count = mode_field.shape[1]
    row_count = mode_field.shape[2]
    col_count = mode_field.shape[3]
    term_count = kl_coeff.shape[0]
    group_count = lax.axis_size("mode")
    all_slots = slot_count * group_count
    my_group = lax.axis_index("mode")
    first_slot = my_group * slot_count
    mode_count = mode_slot.shape[0]
    mode_labels = lax.broadcasted_iota(jnp.int32, (1, mode_count), 1)
    slot_table = mode_slot[None, :]
    slot_in = jnp.sum(jnp.where(trip_in[:, None] == mode_labels, slot_table, 0), axis=1)
    slot_out = jnp.sum(jnp.where(trip_out[:, None] == mode_labels, slot_table, 0), axis=1)
    local_out = slot_out - first_slot
    is_owned = (local_out >= 0) & (local_out < slot_count)
    row_index = trip_kl * slot_count + jnp.clip(local_out, 0, slot_count - 1)
    weights = jnp.where(is_owned, trip_weight.astype(jnp.float32), 0.0)
    coupling = (
        jnp.zeros((term_count * slot_count, all_slots), jnp.float32)
        .at[row_index, slot_in]
        .add(weights)
    )
    coupling = coupling.astype(jnp.bfloat16)
    coeff_rim = padded(kl_coeff, (("space", 1),), 1)
    field_rim = padded(mode_field, (("space", 1),), 1)
    shard_part = lax.all_gather(field_rim, "mode", axis=0, tiled=True)
    flat_rows = shard_part.reshape(shard_part.shape[0], -1)
    combined = jnp.dot(coupling, flat_rows, preferred_element_type=jnp.float32)
    combined = combined.reshape(term_count, slot_count, plane_count + 2, row_count, col_count)
    side_pad = ((0, 0), (0, 0), (1, 1), (1, 1))
    coeff_pad = jnp.pad(coeff_rim, side_pad)
    response = jnp.zeros((slot_count, plane_count, row_count, col_count), jnp.float32)
    for term_index in range(term_count):
        response = response + diffusion(
            jnp.pad(combined[term_index], side_pad), coeff_pad[term_index]
        )
    return response


def solution(mesh):
    placed = (P("mode", "space", None, None), P(None, "space", None, None), P(), P(), P(), P(), P())
    return jax.shard_map(
        body, mesh=mesh, in_specs=placed, out_specs=P("mode", "space", None, None), check_vma=False
    )
```

profile of v0, /device:TPU:1, one launch (start us, length us, event | category | flops | bytes accessed | tf_op | source)
XLA Modules:
  0.0 106.1 jit_solution(13414980134957937712)
XLA Ops:
  6.5 0.7 fusion.251
  7.3 4.4 %collective-permute-start.2 = (bf16[9,1,8,128]{3,2,1,0:T(8,128)(2,1)S(1)}, bf16[9,1,8,128]{3,2,1,0:T(8,128)(2,1)S(1)}, u32[]{:S(2)}, u32[]{:S(2)}) collective-permute-start(bf16[9,1,8,128]{3,2,1,0:T(8,128)(2,1)S(1)} %get-tuple-element.97), channel_id=1, source_target_pairs={{0,1},{1,2},{2,3},{3,4},{4,5},{5,6},{6,7},{7,8},{8,9},{9,10},{10,1... | collective-permute-start | bytes 55304 | tf_op jit(solution)/shard_map/ppermute | solution.py:14
  11.6 1.3 %collective-permute-start.3 = (bf16[9,1,8,128]{3,2,1,0:T(8,128)(2,1)S(1)}, bf16[9,1,8,128]{3,2,1,0:T(8,128)(2,1)S(1)}, u32[]{:S(2)}, u32[]{:S(2)}) collective-permute-start(bf16[9,1,8,128]{3,2,1,0:T(8,128)(2,1)S(1)} %get-tuple-element.98), channel_id=1, source_target_pairs={{1,0},{2,1},{3,2},{4,3},{5,4},{6,5},{7,6},{8,7},{9,8},{10,9},{11,1... | collective-permute-start | bytes 55304 | tf_op jit(solution)/shard_map/ppermute | solution.py:17
  13.0 3.4 %collective-permute-done.3 = bf16[9,1,8,128]{3,2,1,0:T(8,128)(2,1)S(1)} collective-permute-done((bf16[9,1,8,128]{3,2,1,0:T(8,128)(2,1)S(1)}, bf16[9,1,8,128]{3,2,1,0:T(8,128)(2,1)S(1)}, u32[]{:S(2)}, u32[]{:S(2)}) %collective-permute-start.3) | collective-permute-done | bytes 18464 | tf_op jit(solution)/shard_map/ppermute | solution.py:17
  16.3 1.6 %pad_maximum_fusion = bf16[9,10,8,128]{3,2,1,0:T(8,128)(2,1)} fusion(bf16[9,1,8,128]{3,2,1,0:T(8,128)(2,1)S(1)} %collective-permute-done.3, bf16[9,8,8,128]{3,2,1,0:T(8,128)(2,1)} %param.7, bf16[9,1,8,128]{3,2,1,0:T(8,128)(2,1)S(1)} %collective-permute-done.2), kind=kLoop, calls=%fused_computation.269 | loop fusion | flops 184320 | bytes 368640 | tf_op jit(solution)/shard_map/concatenate | solution.py:18
  18.0 0.8 fusion.250
  18.8 3.5 %collective-permute-start = (f32[11,1,8,128]{3,2,1,0:T(8,128)S(1)}, f32[11,1,8,128]{3,2,1,0:T(8,128)S(1)}, u32[]{:S(2)}, u32[]{:S(2)}) collective-permute-start(f32[11,1,8,128]{3,2,1,0:T(8,128)S(1)} %get-tuple-element.29), channel_id=1, source_target_pairs={{0,1},{1,2},{2,3},{3,4},{4,5},{5,6},{6,7},{7,8},{8,9},{9,10},{10,1... | collective-permute-start | bytes 135176 | tf_op jit(solution)/shard_map/ppermute | solution.py:14
  22.3 1.3 %collective-permute-start.1 = (f32[11,1,8,128]{3,2,1,0:T(8,128)S(1)}, f32[11,1,8,128]{3,2,1,0:T(8,128)S(1)}, u32[]{:S(2)}, u32[]{:S(2)}) collective-permute-start(f32[11,1,8,128]{3,2,1,0:T(8,128)S(1)} %get-tuple-element.30), channel_id=1, source_target_pairs={{1,0},{2,1},{3,2},{4,3},{5,4},{6,5},{7,6},{8,7},{9,8},{10,9},{11,1... | collective-permute-start | bytes 135176 | tf_op jit(solution)/shard_map/ppermute | solution.py:17
  23.6 1.4 %select_reduce_fusion.1 = (s32[1606]{0:T(1024)S(1)}, s32[1606]{0:T(1024)S(1)}) fusion(s32[286]{0:T(512)} %param.9, s32[1606]{0:T(1024)} %param.12, s32[1606]{0:T(1024)} %param.11), kind=kLoop, calls=%fused_computation.54 | loop fusion | flops 2752684 | bytes 26840 | tf_op jit(solution)/shard_map/reduce_sum | solution.py:58
  25.0 0.7 compare_select_fusion.1
  25.7 0.7 multiply_reduce_fusion
  26.5 0.8 and_reduce_fusion
  27.3 0.7 convert_select_fusion
  27.9 10.0 %scatter_custom_fusion = f32[28512]{0:T(1024)S(1)} fusion(s32[1606]{0:T(1024)S(1)} %broadcast_select_fusion, f32[1606]{0:T(1024)S(1)} %convert_select_fusion, f32[]{:T(128)} %constant.9.clone.1), kind=kCustom, calls=%fused_computation.281 | custom fusion | flops 1606 | bytes 114052
  38.0 0.3 reshape.113
  38.3 1.5 %select_maximum_fusion = f32[11,10,10,130]{3,2,1,0:T(8,128)S(1)} fusion(f32[11,1,8,128]{3,2,1,0:T(8,128)S(1)} %collective-permute-done.1, f32[11,8,8,128]{3,2,1,0:T(8,128)} %param.8, f32[11,1,8,128]{3,2,1,0:T(8,128)S(1)} %collective-permute-done), kind=kLoop, calls=%fused_computation.56 | loop fusion | flops 2145000 | bytes 1022560 | tf_op jit(solution)/shard_map/concatenate | solution.py:18
  39.8 0.1 slice_bitcast_fusion.21
  40.0 0.1 fusion.248
  40.1 0.1 fusion.242
  40.2 0.1 fusion.236
  40.3 0.1 fusion.230
  40.5 0.1 fusion.224
  40.6 0.1 fusion.218
  40.7 0.1 fusion.212
  40.8 0.1 fusion.206
  41.0 0.1 fusion.200
  41.1 0.1 fusion.194
  41.2 0.1 fusion.188
  41.3 46.6 %all-gather.2.cloned.1.call-done = bf16[288,10,8,128]{3,2,1,0:T(8,128)(2,1)} async-done(((bf16[9,10,8,128]{3,2,1,0:T(8,128)(2,1)}), bf16[288,10,8,128]{3,2,1,0:T(8,128)(2,1)}) %all-gather.2.cloned.1.call-update) | async-done | bytes 5898256 | tf_op jit(solution)/shard_map/all_gather | solution.py:71
  87.9 4.3 %fusion = f32[99,10240]{1,0:T(8,128)S(1)} fusion(bf16[288,99]{1,0:T(8,128)(2,1)S(1)} %reshape.113, bf16[36,8,80,128]{3,2,1,0:T(8,128)(2,1)} %bitcast.83), kind=kOutput, calls=%fused_computation.1 | convolution fusion | flops 583925760 | bytes 10010304 | tf_op jit(solution)/shard_map/dot_general | solution.py:73
  92.2 0.7 fusion.249
  92.9 0.1 copy.18
  93.0 0.1 copy.19
  93.2 0.1 copy.16
  93.3 0.1 copy.17
  93.5 0.1 copy.14
  93.6 0.1 copy.15
  93.7 0.1 copy.12
  93.9 0.1 copy.13
  94.0 0.1 copy.10
  94.1 0.1 copy.11
  94.3 0.1 copy.9
  94.4 0.1 slice_bitcast_fusion
  94.5 0.1 slice_bitcast_fusion.2
  94.6 0.1 slice_bitcast_fusion.4
  94.6 0.1 slice_bitcast_fusion.6
  94.7 0.1 slice_bitcast_fusion.8
  94.7 4.5 %fusion.21 = f32[9,8,8,128]{3,2,1,0:T(8,128)} fusion(f32[9,10,8,128]{3,2,1,0:T(8,128)S(1)} %slice_bitcast_fusion.10, f32[9,10,8,128]{3,2,1,0:T(8,128)S(1)} %get-tuple-element.108, f32[9,10,8,128]{3,2,1,0:T(8,128)S(1)} %get-tuple-element.107, f32[9,10,8,128]{3,2,1,0:T(8,128)S(1)} %get-tuple-element.106, f32[9,10,8,128]{3,2,1,0:T(8,128)S(1)} %get-tuple-element.105, ...), kind=kLoop, calls=%fused_computation.87 | loop fusion | flops 14524416 | bytes 16244736 | tf_op jit(solution)/shard_map/add | solution.py:79
  (10 shorter events, 0.1 us)
Async XLA Ops:
  6.5 81.4 %all-gather.2.cloned.1.call-start = ((), (), s32[]{:S(2)}) async-start(), calls=%async_computation | async-start | bytes 6082560 | tf_op jit(solution)/shard_map/all_gather | solution.py:71
  7.3 5.7 %collective-permute-start.2 = (bf16[9,1,8,128]{3,2,1,0:T(8,128)(2,1)S(1)}, bf16[9,1,8,128]{3,2,1,0:T(8,128)(2,1)S(1)}, u32[]{:S(2)}, u32[]{:S(2)}) collective-permute-start(bf16[9,1,8,128]{3,2,1,0:T(8,128)(2,1)S(1)} %get-tuple-element.97), channel_id=1, source_target_pairs={{0,1},{1,2},{2,3},{3,4},{4,5},{5,6},{6,7},{7,8},{8,9},{9,10},{10,1... | collective-permute-start | bytes 55304 | tf_op jit(solution)/shard_map/ppermute | solution.py:14
  11.6 4.7 %collective-permute-start.3 = (bf16[9,1,8,128]{3,2,1,0:T(8,128)(2,1)S(1)}, bf16[9,1,8,128]{3,2,1,0:T(8,128)(2,1)S(1)}, u32[]{:S(2)}, u32[]{:S(2)}) collective-permute-start(bf16[9,1,8,128]{3,2,1,0:T(8,128)(2,1)S(1)} %get-tuple-element.98), channel_id=1, source_target_pairs={{1,0},{2,1},{3,2},{4,3},{5,4},{6,5},{7,6},{8,7},{9,8},{10,9},{11,1... | collective-permute-start | bytes 55304 | tf_op jit(solution)/shard_map/ppermute | solution.py:17
  18.8 19.5 %collective-permute-start = (f32[11,1,8,128]{3,2,1,0:T(8,128)S(1)}, f32[11,1,8,128]{3,2,1,0:T(8,128)S(1)}, u32[]{:S(2)}, u32[]{:S(2)}) collective-permute-start(f32[11,1,8,128]{3,2,1,0:T(8,128)S(1)} %get-tuple-element.29), channel_id=1, source_target_pairs={{0,1},{1,2},{2,3},{3,4},{4,5},{5,6},{6,7},{7,8},{8,9},{9,10},{10,1... | collective-permute-start | bytes 135176 | tf_op jit(solution)/shard_map/ppermute | solution.py:14
  22.3 15.9 %collective-permute-start.1 = (f32[11,1,8,128]{3,2,1,0:T(8,128)S(1)}, f32[11,1,8,128]{3,2,1,0:T(8,128)S(1)}, u32[]{:S(2)}, u32[]{:S(2)}) collective-permute-start(f32[11,1,8,128]{3,2,1,0:T(8,128)S(1)} %get-tuple-element.30), channel_id=1, source_target_pairs={{1,0},{2,1},{3,2},{4,3},{5,4},{6,5},{7,6},{8,7},{9,8},{10,9},{11,1... | collective-permute-start | bytes 135176 | tf_op jit(solution)/shard_map/ppermute | solution.py:17
Sparse Core Ops, SparseCore 0:
  18.1 69.7 all-gather.1
where the time goes:
time: 107 us; the launch traced here: 106 us
  waiting for transfers between devices  50 us (47%)
  other arithmetic  23.2 us (22%)
  between operations  13.7 us (13%)
  starting transfers between devices  10.5 us (10%)
  local copies, waits for them, and re-layouts  4.4 us (4%)
  matrix products  4.29 us (4%)
    all_gather x1, waiting for transfers between devices, body(): shard_part = lax.all_gather(field_rim, 'mode', axis=0, tiled=True)  46.6 us
    unnamed x4, other arithmetic  11.5 us
    ppermute x2, starting transfers between devices, padded(): lax.ppermute(lax.slice_in_dim(block, block.shape[dim] - width, None, axis...  7.89 us
    add x1, other arithmetic, body(): response + diffusion(jnp.pad(combined[term_index], side_pad), coeff_pad[t...  4.51 us
    dot_general x1, matrix products, body(): combined = jnp.dot(coupling, flat_rows, preferred_element_type=jnp.float32)  4.29 us
    ppermute x2, waiting for transfers between devices, padded(): lax.ppermute(lax.slice_in_dim(block, 0, width, axis=dim), axis, backward)  3.38 us
    concatenate x2, other arithmetic, padded(): block = jnp.concatenate([low, block, high], axis=dim)  3.14 us
    ppermute x2, starting transfers between devices, padded(): lax.ppermute(lax.slice_in_dim(block, 0, width, axis=dim), axis, backward)  2.58 us
  transfers between devices with their start and end apart: 5, of which 2 were waited for; matrix products, arithmetic and copies ran while one was open for 17% of the time, Pallas kernels for 0%

commit v1 on v0

v1 whole, which is shorter than its diff:
```python
import jax
import jax.numpy as jnp
from jax import lax
from jax.experimental import pallas as pl
from jax.experimental.pallas import tpu as pltpu
from jax.sharding import PartitionSpec as P

MESH = pl.DeviceIdType.MESH
F32 = jnp.float32
BF16 = jnp.bfloat16
NT = (((1,), (1,)), ((), ()))

SIDE = 4
CHIPS = 16
DEVICES = 32
OWN = 9
TERMS = 11
TRIPS = 1606
TRIPS_PAD = 1664
MODES = 286
ROWS = 144
KPAD = 384
MSG = 48
ANS = 40


def iota(shape, dim):
    return lax.broadcasted_iota(jnp.int32, shape, dim)


def lane_of(value):
    return iota(value.shape, value.ndim - 1)


def split(value, parts):
    out = []
    for _ in range(parts):
        piece = value.astype(BF16)
        out.append(piece)
        value = value - piece.astype(F32)
    return out


def yz_sum(value):
    lane = lane_of(value)
    y = lane % 8
    z = (lane // 8) % 8
    total = jnp.where(y > 0, pltpu.roll(value, 1, 1), 0.0)
    total = total + jnp.where(y < 7, pltpu.roll(value, 127, 1), 0.0)
    total = total + jnp.where(z > 0, pltpu.roll(value, 8, 1), 0.0)
    return total + jnp.where(z < 7, pltpu.roll(value, 120, 1), 0.0)


def x_sum(tiles, j):
    lane = lane_of(tiles(0))
    left = tiles(j - 1) if j > 0 else jnp.where(lane >= 64, pltpu.roll(tiles(3), 64, 1), 0.0)
    right = tiles(j + 1) if j < 3 else jnp.where(lane < 64, pltpu.roll(tiles(0), 64, 1), 0.0)
    return left + right


def column_select(rows, chip, half, j):
    target = 8 * chip + j + 4 * half
    target = jnp.where(j == 4, jnp.where(half == 0, 8 * chip - 1, 8 * chip + 8), target)
    target = jnp.where(j > 4, -1, target)
    return jnp.where(iota((rows, 128), 1) == target, 1.0, 0.0).astype(BF16)


def edge_gather():
    row = iota((512, 128), 0)
    out = iota((512, 128), 1)
    j, half, z, y = row // 128, (row // 64) % 2, (row // 8) % 8, row % 8
    place = (j + 4 * half) * 8 + y
    hit = ((z == 0) & (out == place)) | ((z == 7) & (out == 64 + place))
    return jnp.where(hit, 1.0, 0.0).astype(BF16)


def edge_spread():
    out = iota((128, 512), 1)
    row = iota((128, 512), 0)
    j, half, z, y = out // 128, (out // 64) % 2, (out // 8) % 8, out % 8
    place = (j + 4 * half) * 8 + y
    hit = ((z == 7) & (row == place)) | ((z == 0) & (row == 64 + place))
    return jnp.where(hit, 1.0, 0.0).astype(BF16)


def kernel(
    v_ref, k_ref, slot_ref, kl_ref, in_ref, out_ref, w_ref, o_ref,
    pack, msg, got, ninth, vf, vb, svb, onehot, cc, wbuf, ubuf, hbuf,
    kt, ka, eok, kzi, hxc, hzc, eo, ezi, ra, bb, ex, ez, ans, ret, turn, places, trip, table,
    send1, recv1, sendk, recvk, sendz, recvz, send2, recv2,
):
    me = lax.axis_index("mode")
    zi = lax.axis_index("space")
    nz = lax.axis_size("space")
    chip, core = me // 2, me % 2
    ypos, xpos = chip // SIDE, chip % SIDE

    offsets = [
        (ky, kx, kc) for ky in range(SIDE) for kx in range(SIDE) for kc in range(2) if (ky, kx, kc) != (0, 0, 0)
    ]
    offsets.sort(key=lambda o: -(min(o[0], SIDE - o[0]) + min(o[1], SIDE - o[1])))

    def chip_at(ky, kx):
        return lax.rem(ypos + ky, SIDE) * SIDE + lax.rem(xpos + kx, SIDE)

    up, down = lax.rem(zi + 1, nz), lax.rem(zi + nz - 1, nz)

    barrier = pltpu.get_barrier_semaphore()
    for ky, kx, kc in offsets:
        pl.semaphore_signal(
            barrier, inc=1, device_id=(chip_at(ky, kx) * 2 + lax.rem(core + kc, 2), zi), device_id_type=MESH
        )
    for other in (up, down):
        pl.semaphore_signal(barrier, inc=1, device_id=(me, other), device_id_type=MESH)

    row = iota((256, 128), 0)
    select = column_select(256, (row % 128) // 8, row // 128, row % 8)
    low = iota((128, 128), 1) < 64
    for m in range(OWN):
        field = v_ref[m].astype(F32).reshape(64, 128)
        field = jnp.concatenate([field, field], axis=0).astype(BF16)
        turned = lax.dot_general(select, field, NT, preferred_element_type=F32)
        turned = jnp.where(low, turned[:128], turned[128:])
        for c in range(CHIPS):
            if m < 8:
                pack[pl.ds(c * 64 + m, 8, stride=8), :] = turned[c * 8 : c * 8 + 8]
            else:
                pack[pl.ds(c * 64 + 40, 8), :] = turned[c * 8 : c * 8 + 8]
    for c in range(CHIPS):
        msg[c] = pack[pl.ds(c * 64, MSG), :].astype(BF16)
    got[pl.ds(me, 1)] = msg[pl.ds(chip, 1)]

    pl.semaphore_wait(barrier, len(offsets) + 2)
    for ky, kx, kc in offsets:
        target = chip_at(ky, kx)
        pltpu.make_async_remote_copy(
            src_ref=msg.at[target], dst_ref=got.at[me], send_sem=send1, recv_sem=recv1,
            device_id=(target * 2 + lax.rem(core + kc, 2), zi), device_id_type=MESH,
        ).start()

    gather_edge = edge_gather()
    spread_edge = edge_spread()
    kt[...] = jnp.zeros_like(kt)
    row16 = iota((16, 128), 0)
    select_k = column_select(16, chip, row16 // 8, row16 % 8)
    for i in range(TERMS):
        block = k_ref[i].reshape(64, 128)
        block = jnp.concatenate([block, block], axis=0)
        turned = jnp.zeros((16, 128), F32)
        for piece in reversed(split(block, 3)):
            turned = turned + lax.dot_general(select_k, piece, NT, preferred_element_type=F32)
        kt[pl.ds(i, 8, stride=16), :] = jnp.where(low[:8], turned[:8], turned[8:])

    def k_tile(j):
        return kt[j * 16 : j * 16 + 16, :]

    whole = jnp.concatenate([k_tile(j) for j in range(4)], axis=1)
    edge = jnp.zeros((16, 128), F32)
    for piece in reversed(split(whole, 3)):
        edge = edge + jnp.dot(piece, gather_edge, preferred_element_type=F32)
    eok[...] = edge
    k_copies = []
    for n, other in enumerate((down, up)):
        copy = pltpu.make_async_remote_copy(
            src_ref=eok, dst_ref=kzi.at[n], send_sem=sendk.at[n], recv_sem=recvk.at[n],
            device_id=(me, other), device_id_type=MESH,
        )
        copy.start()
        k_copies.append(copy)

    trip[...] = jnp.full(trip.shape, -1, jnp.int32)
    trip[0:1, 0:TRIPS] = in_ref[...]
    trip[1:2, 0:TRIPS] = out_ref[...]
    trip[2:3, 0:TRIPS] = kl_ref[...]
    table[...] = jnp.zeros(table.shape, F32)
    table[0:1, 0:TRIPS] = w_ref[...].astype(F32)
    slots = jnp.broadcast_to(slot_ref[...], (16, MODES))
    dev = lax.shift_right_logical(slots * 57, 9)
    kind = slots - dev * OWN
    column = jnp.where(kind < 8, dev * 8 + kind, 256 + dev)
    place = jnp.where(kind < 8, (dev // 2) * 8 + kind, 128 + dev // 2)
    place = jnp.where(dev % 2 == core, place, 240)
    row16m = iota((16, MODES), 0)
    number = jnp.where(row16m < 2, column, place)
    digits = jnp.where(row16m % 2 == 0, lax.shift_right_logical(number, 4), number & 15)
    digits = jnp.where(row16m < 4, digits, 0).astype(F32)
    places[...] = jnp.zeros((16, KPAD), F32)
    places[:, 0:MODES] = digits
    digits = places[...].astype(BF16)
    mode_row = iota((KPAD, TRIPS_PAD), 0)
    hit_in = jnp.where(mode_row == trip[0:1, :], 1.0, 0.0).astype(BF16)
    look_in = jnp.dot(digits, hit_in, preferred_element_type=F32)
    hit_out = jnp.where(mode_row == trip[1:2, :], 1.0, 0.0).astype(BF16)
    look_out = jnp.dot(digits, hit_out, preferred_element_type=F32)
    column_t = (look_in[0:1] * 16.0 + look_in[1:2]).astype(jnp.int32)
    place_t = (look_out[2:3] * 16.0 + look_out[3:4]).astype(jnp.int32)
    key_t = jnp.where(place_t < ROWS, trip[2:3, :] * ROWS + place_t, -1)
    trip[3:4, :] = key_t
    by_column = jnp.where(mode_row == column_t, 1.0, 0.0).astype(BF16)

    @pl.loop(0, TERMS)
    def _(i):
        rows = iota((ROWS, TRIPS_PAD), 0) + i * ROWS
        part = jnp.where(rows == trip[3:4, :], table[0:1, :], 0.0).astype(BF16)
        onehot[pl.ds(pl.multiple_of(i * ROWS, 16), ROWS), :] = part

    coupling = lax.dot_general(onehot[...], by_column, NT, preferred_element_type=F32).astype(BF16)
    cc[:, 0:KPAD] = coupling
    cc[:, KPAD:] = coupling

    for copy in k_copies:
        copy.wait()
    lane16 = iota((16, 128), 1)
    inside_up = jnp.where(zi < nz - 1, 1.0, 0.0)
    inside_down = jnp.where(zi > 0, 1.0, 0.0)
    k_beyond = jnp.where(lane16 < 64, kzi[0] * inside_up, kzi[1] * inside_down)
    hzc[...] = pltpu.roll(edge, 64, 1) + k_beyond
    hxc[...] = jnp.where(lane16 < 64, k_tile(0), k_tile(3)) + k_tile(4)
    spread = jnp.zeros((16, 512), F32)
    for piece in reversed(split(k_beyond, 3)):
        spread = spread + jnp.dot(piece, spread_edge, preferred_element_type=F32)
    for j in range(4):
        total = 6.0 * k_tile(j) + x_sum(k_tile, j) + yz_sum(k_tile(j)) + spread[:, j * 128 : j * 128 + 128]
        if j == 0:
            total = total + jnp.where(lane16 < 64, k_tile(4), 0.0)
        if j == 3:
            total = total + jnp.where(lane16 >= 64, k_tile(4), 0.0)
        ka[j] = total

    vb[288:KPAD, :] = jnp.zeros((KPAD - 288, 768), BF16)
    svb[288:KPAD, :] = jnp.zeros((KPAD - 288, 512), BF16)
    svb[KPAD + 288 :, :] = jnp.zeros((KPAD - 288, 512), BF16)

    pltpu.make_async_copy(got.at[pl.ds(0, DEVICES - 1)], got.at[pl.ds(0, DEVICES - 1)], recv1).wait()
    for pair in range(3):
        both = got[:, pair * 16 : pair * 16 + 16, :].astype(F32)
        first, second = both[:, :8, :].reshape(256, 128), both[:, 8:, :].reshape(256, 128)
        vf[pair * 2, 0:256, :] = first
        if pair < 2:
            vf[pair * 2 + 1, 0:256, :] = second
        else:
            ninth[...] = second
    for j in range(5):
        vf[j, 256:288, :] = ninth[pl.ds(j, 32, stride=8), :]
        vb[0:288, j * 128 : j * 128 + 128] = vf[j].astype(BF16)

    edge_v = jnp.dot(vb[0:288, 0:512], gather_edge, preferred_element_type=F32)
    eo[...] = edge_v.astype(BF16)
    z_copies = []
    for n, other in enumerate((down, up)):
        copy = pltpu.make_async_remote_copy(
            src_ref=eo, dst_ref=ezi.at[n], send_sem=sendz.at[n], recv_sem=recvz.at[n],
            device_id=(me, other), device_id_type=MESH,
        )
        copy.start()
        z_copies.append(copy)

    wbuf[...] = jnp.dot(cc[:, 0:KPAD], vb[:, 0:512], preferred_element_type=F32)

    p0, p1 = iota((128, 128), 0), iota((128, 128), 1)
    dz, dy = (p0 // 8) % 8 - (p1 // 8) % 8, p0 % 8 - p1 % 8
    near = (p0 // 64 == p1 // 64) & (dz * dz + dy * dy == 1)
    near = jnp.where(near, 1.0, 0.0).astype(BF16)
    for j in range(4):
        total = jnp.dot(vb[0:288, j * 128 : j * 128 + 128], near, preferred_element_type=F32)
        total = total + x_sum(lambda n: vf[n], j)
        high, rest = split(total, 2)
        svb[0:288, j * 128 : j * 128 + 128] = high
        svb[KPAD : KPAD + 288, j * 128 : j * 128 + 128] = rest
    ubuf[...] = jnp.dot(cc[...], svb[...], preferred_element_type=F32)

    for copy in z_copies:
        copy.wait()
    lane288 = iota((288, 128), 1)
    beyond = jnp.where(lane288 < 64, ezi[0].astype(F32) * inside_up, ezi[1].astype(F32) * inside_down)
    vb[0:288, 640:768] = beyond.astype(BF16)
    hbuf[...] = jnp.dot(cc[:, 0:KPAD], vb[:, 512:768], preferred_element_type=F32)

    @pl.loop(0, ROWS // 16)
    def _(block):
        acc = [jnp.zeros((16, 128), F32) for _ in range(4)]
        mass = [jnp.zeros((16, 128), F32) for _ in range(4)]
        side = jnp.zeros((16, 128), F32)
        ends = jnp.zeros((16, 128), F32)
        for i in range(TERMS):
            at = pl.ds(pl.multiple_of(i * ROWS + block * 16, 16), 16)
            for j in range(4):
                k_row = kt[j * 16 + i : j * 16 + i + 1, :]
                w = wbuf[at, j * 128 : j * 128 + 128]
                acc[j] = acc[j] + ka[j, i : i + 1, :] * w - k_row * ubuf[at, j * 128 : j * 128 + 128]
                mass[j] = mass[j] + k_row * w
            side = side + hxc[i : i + 1, :] * hbuf[at, 0:128]
            ends = ends + hzc[i : i + 1, :] * hbuf[at, 128:256]
        here = pl.ds(pl.multiple_of(block * 16, 16), 16)
        for j in range(4):
            ra[j, here, :] = acc[j]
            bb[j, here, :] = mass[j]
        ex[here, :] = side
        ez[here, :] = ends

    end_parts = jnp.zeros((ROWS, 512), F32)
    for piece in reversed(split(ez[...], 2)):
        end_parts = end_parts + jnp.dot(piece, spread_edge, preferred_element_type=F32)
    lane = iota((ROWS, 128), 1)
    for j in range(4):
        total = ra[j] - x_sum(lambda n: bb[n], j) - yz_sum(bb[j]) - end_parts[:, j * 128 : j * 128 + 128]
        if j == 0:
            total = total - jnp.where(lane < 64, ex[...], 0.0)
        if j == 3:
            total = total - jnp.where(lane >= 64, ex[...], 0.0)
        total = 0.5 * total
        for c in range(CHIPS):
            ans[c * ANS + j * 8 : c * ANS + j * 8 + 8, :] = total[c * 8 : c * 8 + 8]
        ans[pl.ds(32 + j, CHIPS, stride=ANS), :] = total[128:ROWS]
    for j in range(4, 8):
        ans[pl.ds(32 + j, CHIPS, stride=ANS), :] = jnp.zeros((CHIPS, 128), F32)

    def block_of(c):
        return pl.ds(pl.multiple_of(c * ANS, 8), ANS)

    for ky, kx, kc in offsets:
        if kc == 0:
            target = chip_at(ky, kx)
            pltpu.make_async_remote_copy(
                src_ref=ans.at[block_of(target), :], dst_ref=ret.at[block_of(chip), :], send_sem=send2, recv_sem=recv2,
                device_id=(target * 2 + core, zi), device_id_type=MESH,
            ).start()
    ret[block_of(chip), :] = ans[block_of(chip), :]
    rest = ret.at[pl.ds(0, (CHIPS - 1) * ANS), :]
    pltpu.make_async_copy(rest, rest, recv2).wait()

    low16 = iota((CHIPS, 128), 1) < 64
    for first in range(0, OWN, 2):
        second = min(first + 1, OWN - 1)
        for j in range(4):
            one = ret[pl.ds(j * 8 + first if first < 8 else 32 + j, CHIPS, stride=ANS), :]
            two = ret[pl.ds(j * 8 + second if second < 8 else 32 + j, CHIPS, stride=ANS), :]
            turn[pl.ds(j, CHIPS, stride=8), :] = jnp.where(low16, one, pltpu.roll(two, 64, 1))
            turn[pl.ds(4 + j, CHIPS, stride=8), :] = jnp.where(low16, pltpu.roll(one, 64, 1), two)
        turned = turn[...].T
        o_ref[first] = turned[:64].reshape(8, 8, 128)
        if second > first:
            o_ref[second] = turned[64:].reshape(8, 8, 128)

    pltpu.make_async_copy(got.at[pl.ds(0, DEVICES - 1)], got.at[pl.ds(0, DEVICES - 1)], send1).wait()
    pltpu.make_async_copy(rest, rest, send2).wait()


def body(mode_field, kl_coeff, mode_slot, trip_kl, trip_in, trip_out, trip_weight):
    vmem = pl.BlockSpec(memory_space=pltpu.VMEM)
    dma = pltpu.SemaphoreType.DMA
    call = pl.pallas_call(
        kernel,
        out_shape=jax.ShapeDtypeStruct(mode_field.shape, F32),
        in_specs=[vmem] * 7,
        out_specs=vmem,
        scratch_shapes=[
            pltpu.VMEM((CHIPS * 64, 128), F32),
            pltpu.VMEM((CHIPS, MSG, 128), BF16),
            pltpu.VMEM((DEVICES, MSG, 128), BF16),
            pltpu.VMEM((256, 128), F32),
            pltpu.VMEM((5, 288, 128), F32),
            pltpu.VMEM((KPAD, 768), BF16),
            pltpu.VMEM((2 * KPAD, 512), BF16),
            pltpu.VMEM((TERMS * ROWS, TRIPS_PAD), BF16),
            pltpu.VMEM((TERMS * ROWS, 2 * KPAD), BF16),
            pltpu.VMEM((TERMS * ROWS, 512), F32),
            pltpu.VMEM((TERMS * ROWS, 512), F32),
            pltpu.VMEM((TERMS * ROWS, 256), F32),
            pltpu.VMEM((128, 128), F32),
            pltpu.VMEM((4, 16, 128), F32),
            pltpu.VMEM((16, 128), F32),
            pltpu.VMEM((2, 16, 128), F32),
            pltpu.VMEM((16, 128), F32),
            pltpu.VMEM((16, 128), F32),
            pltpu.VMEM((288, 128), BF16),
            pltpu.VMEM((2, 288, 128), BF16),
            pltpu.VMEM((4, ROWS, 128), F32),
            pltpu.VMEM((4, ROWS, 128), F32),
            pltpu.VMEM((ROWS, 128), F32),
            pltpu.VMEM((ROWS, 128), F32),
            pltpu.VMEM((CHIPS * ANS, 128), F32),
            pltpu.VMEM((CHIPS * ANS, 128), F32),
            pltpu.VMEM((128, 128), F32),
            pltpu.VMEM((16, KPAD), F32),
            pltpu.VMEM((8, TRIPS_PAD), jnp.int32),
            pltpu.VMEM((8, TRIPS_PAD), F32),
            dma, dma, dma((2,)), dma((2,)), dma((2,)), dma((2,)), dma, dma,
        ],
        compiler_params=pltpu.CompilerParams(
            collective_id=0, has_side_effects=True, vmem_limit_bytes=48 << 20
        ),
    )
    return call(
        mode_field, kl_coeff, mode_slot[None, :], trip_kl[None, :], trip_in[None, :], trip_out[None, :],
        trip_weight[None, :],
    )


def solution(mesh):
    placed = (P("mode", "space", None, None), P(None, "space", None, None), P(), P(), P(), P(), P())
    return jax.shard_map(
        body, mesh=mesh, in_specs=placed, out_specs=P("mode", "space", None, None), check_vma=False
    )
```

time: 107 us -> 40.4 us (0.38)
  waiting for transfers between devices: 50 us -> 0 us
  Pallas kernels: 0 us -> 34.7 us
  other arithmetic: 23.2 us -> 0 us
  between operations: 13.7 us -> 0.03 us
  starting transfers between devices: 10.5 us -> 0 us
  matrix products: 4.29 us -> 0 us
    all_gather x1 -> x0, waiting for transfers between devices: 46.6 us -> none  [body(): shard_part = lax.all_gather(field_rim, 'mode', axis=0, tiled=True)]
    pallas_call x0 -> x1, Pallas kernels: none -> 34.7 us  [body(): call(mode_field, kl_coeff, mode_slot[None, :], trip_kl[None, :], trip_in[...]
    unnamed x4 -> x0, other arithmetic: 11.5 us -> none
    ppermute x4 -> x0, starting transfers between devices: 10.5 us -> none  [the longest x2 7.89 us: padded(): lax.ppermute(lax.slice_in_dim(block, block.shape[dim] - width, None, axis...]
    add x1 -> x0, other arithmetic: 4.51 us -> none  [body(): response + diffusion(jnp.pad(combined[term_index], side_pad), coeff_pad[t...]
    dot_general x1 -> x0, matrix products: 4.29 us -> none  [body(): combined = jnp.dot(coupling, flat_rows, preferred_element_type=jnp.float32)]
    ppermute x4 -> x0, waiting for transfers between devices: 3.39 us -> none  [the longest x2 3.38 us: padded(): lax.ppermute(lax.slice_in_dim(block, 0, width, axis=dim), axis, backward)]
    concatenate x2 -> x0, other arithmetic: 3.14 us -> none  [padded(): block = jnp.concatenate([low, block, high], axis=dim)]
  transfers between devices with their start and end apart: 5 -> 0, of which waited for: 2 -> 0; matrix products, arithmetic and copies ran while one was open for 17% -> 0% of each run, Pallas kernels for 0% -> 0%
where the time goes in v1:
time: 40.4 us; the launch traced here: 40.1 us
  Pallas kernels  34.7 us (86%)
  local copies, waits for them, and re-layouts  5.38 us (13%)
    pallas_call x1, Pallas kernels, body(): call(mode_field, kl_coeff, mode_slot[None, :], trip_kl[None, :], trip_in[...  34.7 us
    unnamed x11, local copies, waits for them, and re-layouts  3.97 us

profile of v1, /device:TPU:1, one launch (start us, length us, event | category | flops | bytes accessed | tf_op | source)
XLA Modules:
  0.0 40.1 jit_solution(11889138676293567624)
XLA Ops:
  0.0 0.7 %broadcast_in_dim.15.slot_ref = s32[1,286]{1,0:T(1,128)S(1)} reshape(s32[286]{0:T(512)} %param.9) | data formatting | bytes 2288 | tf_op jit(solution)/shard_map/broadcast_in_dim | solution.py:395
  0.7 0.0 copy-start.2
  0.7 0.7 %broadcast_in_dim.16.kl_ref = s32[1,1606]{1,0:T(1,128)S(1)} reshape(s32[1606]{0:T(1024)} %param.10) | data formatting | bytes 12848 | tf_op jit(solution)/shard_map/broadcast_in_dim | solution.py:395
  1.4 0.0 copy-done.2
  1.4 0.0 copy-start.3
  1.4 0.7 %copy-done.3 = s32[1606]{0:T(1024)S(1)} copy-done((s32[1606]{0:T(1024)S(1)}, s32[1606]{0:T(1024)}, u32[]{:S(2)}) %copy-start.3) | copy-done | bytes 6448
  2.1 0.0 copy-start.4
  2.1 0.7 %copy-done.4 = bf16[1606]{0:T(1024)(128)(2,1)S(1)} copy-done((bf16[1606]{0:T(1024)(128)(2,1)S(1)}, bf16[1606]{0:T(1024)(128)(2,1)}, u32[]{:S(2)}) %copy-start.4) | copy-done | bytes 3236
  2.8 0.0 copy-start
  2.8 1.0 %copy-done = f32[11,8,8,128]{3,2,1,0:T(8,128)S(1)} copy-done((f32[11,8,8,128]{3,2,1,0:T(8,128)S(1)}, f32[11,8,8,128]{3,2,1,0:T(8,128)}, u32[]{:S(2)}) %copy-start) | copy-done | bytes 360472
  3.8 0.0 copy-start.1
  3.8 0.9 %copy-done.1 = bf16[9,8,8,128]{3,2,1,0:T(8,128)(2,1)S(1)} copy-done((bf16[9,8,8,128]{3,2,1,0:T(8,128)(2,1)S(1)}, bf16[9,8,8,128]{3,2,1,0:T(8,128)(2,1)}, u32[]{:S(2)}) %copy-start.1) | copy-done | bytes 147480
  4.7 34.7 %shard_map.73 = f32[9,8,8,128]{3,2,1,0:T(8,128)S(1)} custom-call(bf16[9,8,8,128]{3,2,1,0:T(8,128)(2,1)S(1)} %copy-done.1, f32[11,8,8,128]{3,2,1,0:T(8,128)S(1)} %copy-done, s32[1,286]{1,0:T(1,128)S(1)} %broadcast_in_dim.15.slot_ref, s32[1,1606]{1,0:T(1,128)S(1)} %broadcast_in_dim.16.kl_ref, s32[1,1606]{1,0:T(1,128)S(1)} %broadcast_in_dim.17.in_ref, ...), custom_call_target="tpu_custom_call" | custom-call | tf_op jit(solution)/shard_map/pallas_call | solution.py:394
  39.4 0.7 %copy.9 = f32[9,8,8,128]{3,2,1,0:T(8,128)} copy(f32[9,8,8,128]{3,2,1,0:T(8,128)S(1)} %shard_map.73) | data formatting | bytes 589824
  (3 shorter events, 0.0 us)
Async XLA Ops:
  0.7 0.7 %copy-start.2 = (s32[1606]{0:T(1024)S(1)}, s32[1606]{0:T(1024)}, u32[]{:S(2)}) copy-start(s32[1606]{0:T(1024)} %param.11) | copy-start | bytes 19276
  1.4 0.7 %copy-start.3 = (s32[1606]{0:T(1024)S(1)}, s32[1606]{0:T(1024)}, u32[]{:S(2)}) copy-start(s32[1606]{0:T(1024)} %param.12) | copy-start | bytes 19276
  2.1 0.7 %copy-start.4 = (bf16[1606]{0:T(1024)(128)(2,1)S(1)}, bf16[1606]{0:T(1024)(128)(2,1)}, u32[]{:S(2)}) copy-start(bf16[1606]{0:T(1024)(128)(2,1)} %param.13) | copy-start | bytes 9640
  2.8 1.0 %copy-start = (f32[11,8,8,128]{3,2,1,0:T(8,128)S(1)}, f32[11,8,8,128]{3,2,1,0:T(8,128)}, u32[]{:S(2)}) copy-start(f32[11,8,8,128]{3,2,1,0:T(8,128)} %k_ref.1) | copy-start | bytes 1081348
  3.8 0.9 %copy-start.1 = (bf16[9,8,8,128]{3,2,1,0:T(8,128)(2,1)S(1)}, bf16[9,8,8,128]{3,2,1,0:T(8,128)(2,1)}, u32[]{:S(2)}) copy-start(bf16[9,8,8,128]{3,2,1,0:T(8,128)(2,1)} %v_ref.1) | copy-start | bytes 442372

commit v2 on v1

--- a/solution.py
+++ b/solution.py
@@ -12,7 +12,6 @@
 
 SIDE = 4
 CHIPS = 16
-DEVICES = 32
 OWN = 9
 TERMS = 11
 TRIPS = 1606
@@ -84,20 +83,28 @@
 
 
 def kernel(
-    v_ref, k_ref, slot_ref, kl_ref, in_ref, out_ref, w_ref, o_ref,
-    pack, msg, got, ninth, vf, vb, svb, onehot, cc, wbuf, ubuf, hbuf,
+    v_hbm, k_hbm, slot_hbm, kl_hbm, in_hbm, out_hbm, w_hbm, o_ref,
+    v_ref, k_ref, slot_ref, kl_ref, in_ref, out_ref, w_ref,
+    pack, msg, got, ninth, vf, vb, svb, onehot, cc, wbuf, ubuf, hbuf, main,
     kt, ka, eok, kzi, hxc, hzc, eo, ezi, ra, bb, ex, ez, ans, ret, turn, places, trip, table,
-    send1, recv1, sendk, recvk, sendz, recvz, send2, recv2,
+    load, send1, recv1, sendr, recvr, sendk, recvk, sendz, recvz, send2, recv2,
 ):
+    loads = [
+        pltpu.make_async_copy(src, dst, load.at[n])
+        for n, (src, dst) in enumerate((
+            (v_hbm, v_ref), (in_hbm, in_ref), (out_hbm, out_ref), (kl_hbm, kl_ref), (slot_hbm, slot_ref),
+            (w_hbm, w_ref), (k_hbm, k_ref),
+        ))
+    ]
+    loads[0].start()
+
     me = lax.axis_index("mode")
     zi = lax.axis_index("space")
     nz = lax.axis_size("space")
     chip, core = me // 2, me % 2
     ypos, xpos = chip // SIDE, chip % SIDE
 
-    offsets = [
-        (ky, kx, kc) for ky in range(SIDE) for kx in range(SIDE) for kc in range(2) if (ky, kx, kc) != (0, 0, 0)
-    ]
+    offsets = [(ky, kx) for ky in range(SIDE) for kx in range(SIDE) if (ky, kx) != (0, 0)]
     offsets.sort(key=lambda o: -(min(o[0], SIDE - o[0]) + min(o[1], SIDE - o[1])))
 
     def chip_at(ky, kx):
@@ -106,16 +113,21 @@
     up, down = lax.rem(zi + 1, nz), lax.rem(zi + nz - 1, nz)
 
     barrier = pltpu.get_barrier_semaphore()
-    for ky, kx, kc in offsets:
-        pl.semaphore_signal(
-            barrier, inc=1, device_id=(chip_at(ky, kx) * 2 + lax.rem(core + kc, 2), zi), device_id_type=MESH
-        )
-    for other in (up, down):
-        pl.semaphore_signal(barrier, inc=1, device_id=(me, other), device_id_type=MESH)
+    twin = chip * 2 + 1 - core
+    around = [(n, who, other) for n, other in enumerate((down, up)) for who in (me, twin)]
+    for ky, kx in offsets:
+        pl.semaphore_signal(barrier, inc=1, device_id=(chip_at(ky, kx) * 2 + core, zi), device_id_type=MESH)
+    pl.semaphore_signal(barrier, inc=1, device_id=(twin, zi), device_id_type=MESH)
+    for _, who, other in around:
+        pl.semaphore_signal(barrier, inc=1, device_id=(who, other), device_id_type=MESH)
+
+    for copy in loads[1:]:
+        copy.start()
 
     row = iota((256, 128), 0)
     select = column_select(256, (row % 128) // 8, row // 128, row % 8)
     low = iota((128, 128), 1) < 64
+    loads[0].wait()
     for m in range(OWN):
         field = v_ref[m].astype(F32).reshape(64, 128)
         field = jnp.concatenate([field, field], axis=0).astype(BF16)
@@ -128,14 +140,14 @@
                 pack[pl.ds(c * 64 + 40, 8), :] = turned[c * 8 : c * 8 + 8]
     for c in range(CHIPS):
         msg[c] = pack[pl.ds(c * 64, MSG), :].astype(BF16)
-    got[pl.ds(me, 1)] = msg[pl.ds(chip, 1)]
-
-    pl.semaphore_wait(barrier, len(offsets) + 2)
-    for ky, kx, kc in offsets:
+    got[core, 0] = msg[chip]
+
+    pl.semaphore_wait(barrier, len(offsets) + 1 + len(around))
+    for ky, kx in offsets:
         target = chip_at(ky, kx)
         pltpu.make_async_remote_copy(
-            src_ref=msg.at[target], dst_ref=got.at[me], send_sem=send1, recv_sem=recv1,
-            device_id=(target * 2 + lax.rem(core + kc, 2), zi), device_id_type=MESH,
+            src_ref=msg.at[target], dst_ref=got.at[core, ky * SIDE + kx], send_sem=send1, recv_sem=recv1.at[ky],
+            device_id=(target * 2 + core, zi), device_id_type=MESH,
         ).start()
 
     gather_edge = edge_gather()
@@ -143,6 +155,7 @@
     kt[...] = jnp.zeros_like(kt)
     row16 = iota((16, 128), 0)
     select_k = column_select(16, chip, row16 // 8, row16 % 8)
+    loads[6].wait()
     for i in range(TERMS):
         block = k_ref[i].reshape(64, 128)
         block = jnp.concatenate([block, block], axis=0)
@@ -168,16 +181,21 @@
         copy.start()
         k_copies.append(copy)
 
+    for copy in loads[1:6]:
+        copy.wait()
     trip[...] = jnp.full(trip.shape, -1, jnp.int32)
-    trip[0:1, 0:TRIPS] = in_ref[...]
-    trip[1:2, 0:TRIPS] = out_ref[...]
-    trip[2:3, 0:TRIPS] = kl_ref[...]
+    trip[0:1, 0:TRIPS] = in_ref[...].reshape(1, TRIPS)
+    trip[1:2, 0:TRIPS] = out_ref[...].reshape(1, TRIPS)
+    trip[2:3, 0:TRIPS] = kl_ref[...].reshape(1, TRIPS)
     table[...] = jnp.zeros(table.shape, F32)
-    table[0:1, 0:TRIPS] = w_ref[...].astype(F32)
-    slots = jnp.broadcast_to(slot_ref[...], (16, MODES))
+    table[0:1, 0:TRIPS] = w_ref[...].astype(F32).reshape(1, TRIPS)
+    slots = jnp.broadcast_to(slot_ref[...].reshape(1, MODES), (16, MODES))
     dev = lax.shift_right_logical(slots * 57, 9)
     kind = slots - dev * OWN
-    column = jnp.where(kind < 8, dev * 8 + kind, 256 + dev)
+    away_y = (ypos - dev // 8 + SIDE) % SIDE
+    away_x = (xpos - (dev // 2) % SIDE + SIDE) % SIDE
+    came = (dev % 2) * CHIPS + away_y * SIDE + away_x
+    column = jnp.where(kind < 8, came * 8 + kind, 256 + came)
     place = jnp.where(kind < 8, (dev // 2) * 8 + kind, 128 + dev // 2)
     place = jnp.where(dev % 2 == core, place, 240)
     row16m = iota((16, MODES), 0)
@@ -192,11 +210,13 @@
     look_in = jnp.dot(digits, hit_in, preferred_element_type=F32)
     hit_out = jnp.where(mode_row == trip[1:2, :], 1.0, 0.0).astype(BF16)
     look_out = jnp.dot(digits, hit_out, preferred_element_type=F32)
-    column_t = (look_in[0:1] * 16.0 + look_in[1:2]).astype(jnp.int32)
+    look_in = look_in.T
+    column_t = look_in[:, 0:1] * 16.0 + look_in[:, 1:2]
     place_t = (look_out[2:3] * 16.0 + look_out[3:4]).astype(jnp.int32)
     key_t = jnp.where(place_t < ROWS, trip[2:3, :] * ROWS + place_t, -1)
     trip[3:4, :] = key_t
-    by_column = jnp.where(mode_row == column_t, 1.0, 0.0).astype(BF16)
+    lane_number = iota((TRIPS_PAD, KPAD), 1).astype(F32)
+    by_column = jnp.where(lane_number == column_t, 1.0, 0.0).astype(BF16)
 
     @pl.loop(0, TERMS)
     def _(i):
@@ -204,7 +224,7 @@
         part = jnp.where(rows == trip[3:4, :], table[0:1, :], 0.0).astype(BF16)
         onehot[pl.ds(pl.multiple_of(i * ROWS, 16), ROWS), :] = part
 
-    coupling = lax.dot_general(onehot[...], by_column, NT, preferred_element_type=F32).astype(BF16)
+    coupling = jnp.dot(onehot[...], by_column, preferred_element_type=F32).astype(BF16)
     cc[:, 0:KPAD] = coupling
     cc[:, KPAD:] = coupling
 
@@ -231,31 +251,61 @@
     svb[288:KPAD, :] = jnp.zeros((KPAD - 288, 512), BF16)
     svb[KPAD + 288 :, :] = jnp.zeros((KPAD - 288, 512), BF16)
 
-    pltpu.make_async_copy(got.at[pl.ds(0, DEVICES - 1)], got.at[pl.ds(0, DEVICES - 1)], recv1).wait()
-    for pair in range(3):
-        both = got[:, pair * 16 : pair * 16 + 16, :].astype(F32)
-        first, second = both[:, :8, :].reshape(256, 128), both[:, 8:, :].reshape(256, 128)
-        vf[pair * 2, 0:256, :] = first
-        if pair < 2:
-            vf[pair * 2 + 1, 0:256, :] = second
-        else:
-            ninth[...] = second
-    for j in range(5):
-        vf[j, 256:288, :] = ninth[pl.ds(j, 32, stride=8), :]
-        vb[0:288, j * 128 : j * 128 + 128] = vf[j].astype(BF16)
-
-    edge_v = jnp.dot(vb[0:288, 0:512], gather_edge, preferred_element_type=F32)
-    eo[...] = edge_v.astype(BF16)
+    relays = []
+    for ky in (0, 1, 3, 2):
+        first = 1 if ky == 0 else 0
+        here = got.at[core, pl.ds(ky * SIDE + first, SIDE - first)]
+        pltpu.make_async_copy(here, here, recv1.at[ky]).wait()
+        line = got.at[core, pl.ds(ky * SIDE, SIDE)]
+        copy = pltpu.make_async_remote_copy(
+            src_ref=line, dst_ref=line, send_sem=sendr.at[ky], recv_sem=recvr.at[ky],
+            device_id=(twin, zi), device_id_type=MESH,
+        )
+        copy.start()
+        relays.append(copy)
+
+    def unpack(half):
+        most = pl.ds(pl.multiple_of(half * 128, 128), 128)
+        rest = pl.ds(pl.multiple_of(256 + half * 16, 16), 16)
+        for pair in range(3):
+            both = got[half, :, pair * 16 : pair * 16 + 16, :].astype(F32)
+            vf[pair * 2, most, :] = both[:, :8, :].reshape(128, 128)
+            if pair < 2:
+                vf[pair * 2 + 1, most, :] = both[:, 8:, :].reshape(128, 128)
+            else:
+                ninth[...] = both[:, 8:, :].reshape(128, 128)
+        for j in range(5):
+            vf[j, rest, :] = ninth[pl.ds(j, 16, stride=8), :]
+            vb[most, j * 128 : j * 128 + 128] = vf[j, most, :].astype(BF16)
+            vb[rest, j * 128 : j * 128 + 128] = vf[j, rest, :].astype(BF16)
+        return most, rest
+
+    most, rest = unpack(core)
+    edges = jnp.concatenate(
+        [
+            jnp.dot(vb[most, 0:512], gather_edge, preferred_element_type=F32),
+            jnp.dot(vb[rest, 0:512], gather_edge, preferred_element_type=F32),
+            jnp.zeros((16, 128), F32),
+        ],
+        axis=0,
+    )
+    low80 = iota((80, 128), 1) < 64
+    eo[0] = jnp.where(low80, edges[:80], pltpu.roll(edges[80:], 64, 1)).astype(BF16)
+    eo[1] = jnp.where(low80, pltpu.roll(edges[:80], 64, 1), edges[80:]).astype(BF16)
     z_copies = []
-    for n, other in enumerate((down, up)):
+    for n, who, other in around:
+        cross = 0 if who is me else 1
         copy = pltpu.make_async_remote_copy(
-            src_ref=eo, dst_ref=ezi.at[n], send_sem=sendz.at[n], recv_sem=recvz.at[n],
-            device_id=(me, other), device_id_type=MESH,
+            src_ref=eo.at[n], dst_ref=ezi.at[n, core], send_sem=sendz.at[n, cross], recv_sem=recvz.at[n, cross],
+            device_id=(who, other), device_id_type=MESH,
         )
         copy.start()
         z_copies.append(copy)
-
-    wbuf[...] = jnp.dot(cc[:, 0:KPAD], vb[:, 0:512], preferred_element_type=F32)
+    for copy in relays:
+        copy.wait()
+    unpack(1 - core)
+
+    wbuf[...] = jnp.dot(cc[:, 0:KPAD], vb[:, 0:640], preferred_element_type=F32)
 
     p0, p1 = iota((128, 128), 0), iota((128, 128), 1)
     dz, dy = (p0 // 8) % 8 - (p1 // 8) % 8, p0 % 8 - p1 % 8
@@ -269,19 +319,11 @@
         svb[KPAD : KPAD + 288, j * 128 : j * 128 + 128] = rest
     ubuf[...] = jnp.dot(cc[...], svb[...], preferred_element_type=F32)
 
-    for copy in z_copies:
-        copy.wait()
-    lane288 = iota((288, 128), 1)
-    beyond = jnp.where(lane288 < 64, ezi[0].astype(F32) * inside_up, ezi[1].astype(F32) * inside_down)
-    vb[0:288, 640:768] = beyond.astype(BF16)
-    hbuf[...] = jnp.dot(cc[:, 0:KPAD], vb[:, 512:768], preferred_element_type=F32)
-
     @pl.loop(0, ROWS // 16)
     def _(block):
         acc = [jnp.zeros((16, 128), F32) for _ in range(4)]
         mass = [jnp.zeros((16, 128), F32) for _ in range(4)]
         side = jnp.zeros((16, 128), F32)
-        ends = jnp.zeros((16, 128), F32)
         for i in range(TERMS):
             at = pl.ds(pl.multiple_of(i * ROWS + block * 16, 16), 16)
             for j in range(4):
@@ -289,25 +331,47 @@
                 w = wbuf[at, j * 128 : j * 128 + 128]
                 acc[j] = acc[j] + ka[j, i : i + 1, :] * w - k_row * ubuf[at, j * 128 : j * 128 + 128]
                 mass[j] = mass[j] + k_row * w
-            side = side + hxc[i : i + 1, :] * hbuf[at, 0:128]
-            ends = ends + hzc[i : i + 1, :] * hbuf[at, 128:256]
+            side = side + hxc[i : i + 1, :] * wbuf[at, 512:640]
         here = pl.ds(pl.multiple_of(block * 16, 16), 16)
         for j in range(4):
             ra[j, here, :] = acc[j]
             bb[j, here, :] = mass[j]
         ex[here, :] = side
-        ez[here, :] = ends
-
-    end_parts = jnp.zeros((ROWS, 512), F32)
-    for piece in reversed(split(ez[...], 2)):
-        end_parts = end_parts + jnp.dot(piece, spread_edge, preferred_element_type=F32)
+
     lane = iota((ROWS, 128), 1)
     for j in range(4):
-        total = ra[j] - x_sum(lambda n: bb[n], j) - yz_sum(bb[j]) - end_parts[:, j * 128 : j * 128 + 128]
+        total = ra[j] - x_sum(lambda n: bb[n], j) - yz_sum(bb[j])
         if j == 0:
             total = total - jnp.where(lane < 64, ex[...], 0.0)
         if j == 3:
             total = total - jnp.where(lane >= 64, ex[...], 0.0)
+        main[j] = total
+
+    for copy in z_copies:
+        copy.wait()
+    for half in range(2):
+        above = ezi[0, half].astype(F32) * inside_up
+        below = ezi[1, half].astype(F32) * inside_down
+        one = jnp.where(low80, above, pltpu.roll(below, 64, 1)).astype(BF16)
+        two = jnp.where(low80, pltpu.roll(above, 64, 1), below).astype(BF16)
+        vb[half * 128 : half * 128 + 80, 640:768] = one
+        vb[half * 128 + 80 : half * 128 + 128, 640:768] = two[:48]
+        vb[256 + half * 16 : 272 + half * 16, 640:768] = two[48:64]
+    hbuf[...] = jnp.dot(cc[:, 0:KPAD], vb[:, 640:768], preferred_element_type=F32)
+
+    @pl.loop(0, ROWS // 16)
+    def _(block):
+        ends = jnp.zeros((16, 128), F32)
+        for i in range(TERMS):
+            at = pl.ds(pl.multiple_of(i * ROWS + block * 16, 16), 16)
+            ends = ends + hzc[i : i + 1, :] * hbuf[at, :]
+        ez[pl.ds(pl.multiple_of(block * 16, 16), 16), :] = ends
+
+    end_parts = jnp.zeros((ROWS, 512), F32)
+    for piece in reversed(split(ez[...], 2)):
+        end_parts = end_parts + jnp.dot(piece, spread_edge, preferred_element_type=F32)
+    for j in range(4):
+        total = main[j] - end_parts[:, j * 128 : j * 128 + 128]
         total = 0.5 * total
         for c in range(CHIPS):
             ans[c * ANS + j * 8 : c * ANS + j * 8 + 8, :] = total[c * 8 : c * 8 + 8]
@@ -318,13 +382,12 @@
     def block_of(c):
         return pl.ds(pl.multiple_of(c * ANS, 8), ANS)
 
-    for ky, kx, kc in offsets:
-        if kc == 0:
-            target = chip_at(ky, kx)
-            pltpu.make_async_remote_copy(
-                src_ref=ans.at[block_of(target), :], dst_ref=ret.at[block_of(chip), :], send_sem=send2, recv_sem=recv2,
-                device_id=(target * 2 + core, zi), device_id_type=MESH,
-            ).start()
+    for ky, kx in offsets:
+        target = chip_at(ky, kx)
+        pltpu.make_async_remote_copy(
+            src_ref=ans.at[block_of(target), :], dst_ref=ret.at[block_of(chip), :], send_sem=send2, recv_sem=recv2,
+            device_id=(target * 2 + core, zi), device_id_type=MESH,
+        ).start()
     ret[block_of(chip), :] = ans[block_of(chip), :]
     rest = ret.at[pl.ds(0, (CHIPS - 1) * ANS), :]
     pltpu.make_async_copy(rest, rest, recv2).wait()
@@ -342,39 +405,43 @@
         if second > first:
             o_ref[second] = turned[64:].reshape(8, 8, 128)
 
-    pltpu.make_async_copy(got.at[pl.ds(0, DEVICES - 1)], got.at[pl.ds(0, DEVICES - 1)], send1).wait()
+    sent = msg.at[pl.ds(0, CHIPS - 1)]
+    pltpu.make_async_copy(sent, sent, send1).wait()
     pltpu.make_async_copy(rest, rest, send2).wait()
 
 
 def body(mode_field, kl_coeff, mode_slot, trip_kl, trip_in, trip_out, trip_weight):
     vmem = pl.BlockSpec(memory_space=pltpu.VMEM)
+    operands = (mode_field, kl_coeff, mode_slot, trip_kl, trip_in, trip_out, trip_weight)
     dma = pltpu.SemaphoreType.DMA
     call = pl.pallas_call(
         kernel,
         out_shape=jax.ShapeDtypeStruct(mode_field.shape, F32),
-        in_specs=[vmem] * 7,
+        in_specs=[pl.BlockSpec(memory_space=pltpu.HBM)] * 7,
         out_specs=vmem,
         scratch_shapes=[
+            *(pltpu.VMEM(a.shape, a.dtype) for a in operands),
             pltpu.VMEM((CHIPS * 64, 128), F32),
             pltpu.VMEM((CHIPS, MSG, 128), BF16),
-            pltpu.VMEM((DEVICES, MSG, 128), BF16),
-            pltpu.VMEM((256, 128), F32),
+            pltpu.VMEM((2, CHIPS, MSG, 128), BF16),
+            pltpu.VMEM((128, 128), F32),
             pltpu.VMEM((5, 288, 128), F32),
             pltpu.VMEM((KPAD, 768), BF16),
             pltpu.VMEM((2 * KPAD, 512), BF16),
             pltpu.VMEM((TERMS * ROWS, TRIPS_PAD), BF16),
             pltpu.VMEM((TERMS * ROWS, 2 * KPAD), BF16),
+            pltpu.VMEM((TERMS * ROWS, 640), F32),
             pltpu.VMEM((TERMS * ROWS, 512), F32),
-            pltpu.VMEM((TERMS * ROWS, 512), F32),
-            pltpu.VMEM((TERMS * ROWS, 256), F32),
+            pltpu.VMEM((TERMS * ROWS, 128), F32),
+            pltpu.VMEM((4, ROWS, 128), F32),
             pltpu.VMEM((128, 128), F32),
             pltpu.VMEM((4, 16, 128), F32),
             pltpu.VMEM((16, 128), F32),
             pltpu.VMEM((2, 16, 128), F32),
             pltpu.VMEM((16, 128), F32),
             pltpu.VMEM((16, 128), F32),
-            pltpu.VMEM((288, 128), BF16),
-            pltpu.VMEM((2, 288, 128), BF16),
+            pltpu.VMEM((2, 80, 128), BF16),
+            pltpu.VMEM((2, 2, 80, 128), BF16),
             pltpu.VMEM((4, ROWS, 128), F32),
             pltpu.VMEM((4, ROWS, 128), F32),
             pltpu.VMEM((ROWS, 128), F32),
@@ -385,16 +452,13 @@
             pltpu.VMEM((16, KPAD), F32),
             pltpu.VMEM((8, TRIPS_PAD), jnp.int32),
             pltpu.VMEM((8, TRIPS_PAD), F32),
-            dma, dma, dma((2,)), dma((2,)), dma((2,)), dma((2,)), dma, dma,
+            dma((7,)), dma, dma((SIDE,)), dma((SIDE,)), dma((SIDE,)), dma((2,)), dma((2,)), dma((2, 2)), dma((2, 2)), dma, dma,
         ],
         compiler_params=pltpu.CompilerParams(
-            collective_id=0, has_side_effects=True, vmem_limit_bytes=48 << 20
+            collective_id=0, has_side_effects=True, vmem_limit_bytes=40 << 20
         ),
     )
-    return call(
-        mode_field, kl_coeff, mode_slot[None, :], trip_kl[None, :], trip_in[None, :], trip_out[None, :],
-        trip_weight[None, :],
-    )
+    return call(*(pltpu.with_memory_space_constraint(a, pltpu.HBM) for a in operands))
 
 
 def solution(mesh):

time: 40.4 us -> 35 us (0.87)
  local copies, waits for them, and re-layouts: 5.38 us -> 0.72 us
  Pallas kernels: 34.7 us -> 34.2 us
    unnamed x11 -> x1, local copies, waits for them, and re-layouts: 3.97 us -> 0.72 us
    broadcast_in_dim x5 -> x0, local copies, waits for them, and re-layouts: 1.42 us -> none  [the longest x1 0.72 us: body(): trip_kl[None, :]]
    pallas_call x1, Pallas kernels: 34.7 us -> 34.2 us  [body(): call(*(pltpu.with_memory_space_constraint(a, pltpu.HBM) for a in operands))]
where the time goes in v2:
time: 35 us; the launch traced here: 34.9 us
  Pallas kernels  34.2 us (98%)
  local copies, waits for them, and re-layouts  0.72 us (2%)
    pallas_call x1, Pallas kernels, body(): call(*(pltpu.with_memory_space_constraint(a, pltpu.HBM) for a in operands))  34.2 us
    unnamed x1, local copies, waits for them, and re-layouts  0.72 us

profile of v2, /device:TPU:1, one launch (start us, length us, event | category | flops | bytes accessed | tf_op | source)
XLA Modules:
  0.0 34.9 jit_solution(3461562161938979797)
XLA Ops:
  0.0 34.2 %shard_map.73 = f32[9,8,8,128]{3,2,1,0:T(8,128)S(1)} custom-call(bf16[9,8,8,128]{3,2,1,0:T(8,128)(2,1)} %v_hbm.1, f32[11,8,8,128]{3,2,1,0:T(8,128)} %k_hbm.1, s32[286]{0:T(512)} %slot_hbm.1, s32[1606]{0:T(1024)} %kl_hbm.1, s32[1606]{0:T(1024)} %in_hbm.1, s32[1606]{0:T(1024)} %out_hbm.1, bf16[1606]{0:T(1024)(128)(2,1)} %w_hbm.1), custom_call_target="tpu_custom_call" | custom-call | tf_op jit(solution)/shard_map/pallas_call | solution.py:461
  34.2 0.7 %copy.9 = f32[9,8,8,128]{3,2,1,0:T(8,128)} copy(f32[9,8,8,128]{3,2,1,0:T(8,128)S(1)} %shard_map.73) | data formatting | bytes 589824

commit v3 on v2

--- a/solution.py
+++ b/solution.py
@@ -87,7 +87,7 @@
     v_ref, k_ref, slot_ref, kl_ref, in_ref, out_ref, w_ref,
     pack, msg, got, ninth, vf, vb, svb, onehot, cc, wbuf, ubuf, hbuf, main,
     kt, ka, eok, kzi, hxc, hzc, eo, ezi, ra, bb, ex, ez, ans, ret, turn, places, trip, table,
-    load, send1, recv1, sendr, recvr, sendk, recvk, sendz, recvz, send2, recv2,
+    load, ready, send1, recv1, sendr, recvr, sendk, recvk, sendz, recvz, send2, recv2,
 ):
     loads = [
         pltpu.make_async_copy(src, dst, load.at[n])
@@ -118,8 +118,13 @@
     for ky, kx in offsets:
         pl.semaphore_signal(barrier, inc=1, device_id=(chip_at(ky, kx) * 2 + core, zi), device_id_type=MESH)
     pl.semaphore_signal(barrier, inc=1, device_id=(twin, zi), device_id_type=MESH)
-    for _, who, other in around:
-        pl.semaphore_signal(barrier, inc=1, device_id=(who, other), device_id_type=MESH)
+
+    odd = lax.rem(zi, 2)
+
+    @pl.when(odd == 0)
+    def _():
+        for _, who, other in around:
+            pl.semaphore_signal(barrier, inc=1, device_id=(who, other), device_id_type=MESH)
 
     for copy in loads[1:]:
         copy.start()
@@ -142,7 +147,13 @@
         msg[c] = pack[pl.ds(c * 64, MSG), :].astype(BF16)
     got[core, 0] = msg[chip]
 
-    pl.semaphore_wait(barrier, len(offsets) + 1 + len(around))
+    pl.semaphore_wait(barrier, len(offsets) + 1 + len(around) * odd)
+
+    @pl.when(odd == 1)
+    def _():
+        for _, who, other in around:
+            pl.semaphore_signal(ready, inc=1, device_id=(who, other), device_id_type=MESH)
+
     for ky, kx in offsets:
         target = chip_at(ky, kx)
         pltpu.make_async_remote_copy(
@@ -178,8 +189,13 @@
             src_ref=eok, dst_ref=kzi.at[n], send_sem=sendk.at[n], recv_sem=recvk.at[n],
             device_id=(me, other), device_id_type=MESH,
         )
-        copy.start()
         k_copies.append(copy)
+
+    @pl.when(odd == 1)
+    def _():
+        for copy in k_copies:
+            copy.start()
+
 
     for copy in loads[1:6]:
         copy.wait()
@@ -224,32 +240,12 @@
         part = jnp.where(rows == trip[3:4, :], table[0:1, :], 0.0).astype(BF16)
         onehot[pl.ds(pl.multiple_of(i * ROWS, 16), ROWS), :] = part
 
-    coupling = jnp.dot(onehot[...], by_column, preferred_element_type=F32).astype(BF16)
-    cc[:, 0:KPAD] = coupling
-    cc[:, KPAD:] = coupling
-
-    for copy in k_copies:
-        copy.wait()
-    lane16 = iota((16, 128), 1)
-    inside_up = jnp.where(zi < nz - 1, 1.0, 0.0)
-    inside_down = jnp.where(zi > 0, 1.0, 0.0)
-    k_beyond = jnp.where(lane16 < 64, kzi[0] * inside_up, kzi[1] * inside_down)
-    hzc[...] = pltpu.roll(edge, 64, 1) + k_beyond
-    hxc[...] = jnp.where(lane16 < 64, k_tile(0), k_tile(3)) + k_tile(4)
-    spread = jnp.zeros((16, 512), F32)
-    for piece in reversed(split(k_beyond, 3)):
-        spread = spread + jnp.dot(piece, spread_edge, preferred_element_type=F32)
-    for j in range(4):
-        total = 6.0 * k_tile(j) + x_sum(k_tile, j) + yz_sum(k_tile(j)) + spread[:, j * 128 : j * 128 + 128]
-        if j == 0:
-            total = total + jnp.where(lane16 < 64, k_tile(4), 0.0)
-        if j == 3:
-            total = total + jnp.where(lane16 >= 64, k_tile(4), 0.0)
-        ka[j] = total
-
     vb[288:KPAD, :] = jnp.zeros((KPAD - 288, 768), BF16)
     svb[288:KPAD, :] = jnp.zeros((KPAD - 288, 512), BF16)
     svb[KPAD + 288 :, :] = jnp.zeros((KPAD - 288, 512), BF16)
+
+    inside_up = jnp.where(zi < nz - 1, 1.0, 0.0)
+    inside_down = jnp.where(zi > 0, 1.0, 0.0)
 
     relays = []
     for ky in (0, 1, 3, 2):
@@ -279,6 +275,12 @@
             vb[most, j * 128 : j * 128 + 128] = vf[j, most, :].astype(BF16)
             vb[rest, j * 128 : j * 128 + 128] = vf[j, rest, :].astype(BF16)
         return most, rest
+
+    @pl.when(odd == 0)
+    def _():
+        pl.semaphore_wait(ready, len(around))
+        for copy in k_copies:
+            copy.start()
 
     most, rest = unpack(core)
     edges = jnp.concatenate(
@@ -301,23 +303,60 @@
         )
         copy.start()
         z_copies.append(copy)
-    for copy in relays:
-        copy.wait()
-    unpack(1 - core)
-
-    wbuf[...] = jnp.dot(cc[:, 0:KPAD], vb[:, 0:640], preferred_element_type=F32)
-
     p0, p1 = iota((128, 128), 0), iota((128, 128), 1)
     dz, dy = (p0 // 8) % 8 - (p1 // 8) % 8, p0 % 8 - p1 % 8
     near = (p0 // 64 == p1 // 64) & (dz * dz + dy * dy == 1)
     near = jnp.where(near, 1.0, 0.0).astype(BF16)
+
+    def neighbours(rows, low_rows):
+        for j in range(4):
+            total = jnp.dot(vb[rows, j * 128 : j * 128 + 128], near, preferred_element_type=F32)
+            total = total + x_sum(lambda n: vf[n, rows, :], j)
+            high, remainder = split(total, 2)
+            svb[rows, j * 128 : j * 128 + 128] = high
+            svb[low_rows, j * 128 : j * 128 + 128] = remainder
+
+    def shifted_rows(half):
+        return (
+            pl.ds(pl.multiple_of(KPAD + half * 128, 128), 128),
+            pl.ds(pl.multiple_of(KPAD + 256 + half * 16, 16), 16),
+        )
+
+    low_most, low_rest = shifted_rows(core)
+    neighbours(most, low_most)
+    neighbours(rest, low_rest)
+
+    coupling = jnp.dot(onehot[...], by_column, preferred_element_type=F32).astype(BF16)
+    cc[:, 0:KPAD] = coupling
+    cc[:, KPAD:] = coupling
+
+    for copy in relays:
+        copy.wait()
+    most, rest = unpack(1 - core)
+    low_most, low_rest = shifted_rows(1 - core)
+    neighbours(most, low_most)
+    neighbours(rest, low_rest)
+
+    wbuf[...] = jnp.dot(cc[:, 0:KPAD], vb[:, 0:640], preferred_element_type=F32)
+
+    ubuf[...] = jnp.dot(cc[...], svb[...], preferred_element_type=F32)
+
+    for copy in k_copies:
+        copy.wait()
+    lane16 = iota((16, 128), 1)
+    k_beyond = jnp.where(lane16 < 64, kzi[0] * inside_up, kzi[1] * inside_down)
+    hzc[...] = pltpu.roll(edge, 64, 1) + k_beyond
+    hxc[...] = jnp.where(lane16 < 64, k_tile(0), k_tile(3)) + k_tile(4)
+    spread = jnp.zeros((16, 512), F32)
+    for piece in reversed(split(k_beyond, 3)):
+        spread = spread + jnp.dot(piece, spread_edge, preferred_element_type=F32)
     for j in range(4):
-        total = jnp.dot(vb[0:288, j * 128 : j * 128 + 128], near, preferred_element_type=F32)
-        total = total + x_sum(lambda n: vf[n], j)
-        high, rest = split(total, 2)
-        svb[0:288, j * 128 : j * 128 + 128] = high
-        svb[KPAD : KPAD + 288, j * 128 : j * 128 + 128] = rest
-    ubuf[...] = jnp.dot(cc[...], svb[...], preferred_element_type=F32)
+        total = 6.0 * k_tile(j) + x_sum(k_tile, j) + yz_sum(k_tile(j)) + spread[:, j * 128 : j * 128 + 128]
+        if j == 0:
+            total = total + jnp.where(lane16 < 64, k_tile(4), 0.0)
+        if j == 3:
+            total = total + jnp.where(lane16 >= 64, k_tile(4), 0.0)
+        ka[j] = total
 
     @pl.loop(0, ROWS // 16)
     def _(block):
@@ -452,7 +491,7 @@
             pltpu.VMEM((16, KPAD), F32),
             pltpu.VMEM((8, TRIPS_PAD), jnp.int32),
             pltpu.VMEM((8, TRIPS_PAD), F32),
-            dma((7,)), dma, dma((SIDE,)), dma((SIDE,)), dma((SIDE,)), dma((2,)), dma((2,)), dma((2, 2)), dma((2, 2)), dma, dma,
+            dma((7,)), pltpu.SemaphoreType.REGULAR, dma, dma((SIDE,)), dma((SIDE,)), dma((SIDE,)), dma((2,)), dma((2,)), dma((2, 2)), dma((2, 2)), dma, dma,
         ],
         compiler_params=pltpu.CompilerParams(
             collective_id=0, has_side_effects=True, vmem_limit_bytes=40 << 20

time: 35 us -> 33.9 us (0.969)
  Pallas kernels: 34.2 us -> 33.1 us
    pallas_call x1, Pallas kernels: 34.2 us -> 33.1 us  [body(): call(*(pltpu.with_memory_space_constraint(a, pltpu.HBM) for a in operands))]
where the time goes in v3:
time: 33.9 us; the launch traced here: 33.8 us
  Pallas kernels  33.1 us (98%)
  local copies, waits for them, and re-layouts  0.72 us (2%)
    pallas_call x1, Pallas kernels, body(): call(*(pltpu.with_memory_space_constraint(a, pltpu.HBM) for a in operands))  33.1 us
    unnamed x1, local copies, waits for them, and re-layouts  0.72 us

profile of v3, /device:TPU:1, one launch (start us, length us, event | category | flops | bytes accessed | tf_op | source)
XLA Modules:
  0.0 33.8 jit_solution(12099262045662011350)
XLA Ops:
  0.0 33.1 %shard_map.73 = f32[9,8,8,128]{3,2,1,0:T(8,128)S(1)} custom-call(bf16[9,8,8,128]{3,2,1,0:T(8,128)(2,1)} %v_hbm.1, f32[11,8,8,128]{3,2,1,0:T(8,128)} %k_hbm.1, s32[286]{0:T(512)} %slot_hbm.1, s32[1606]{0:T(1024)} %kl_hbm.1, s32[1606]{0:T(1024)} %in_hbm.1, s32[1606]{0:T(1024)} %out_hbm.1, bf16[1606]{0:T(1024)(128)(2,1)} %w_hbm.1), custom_call_target="tpu_custom_call" | custom-call | tf_op jit(solution)/shard_map/pallas_call | solution.py:500
  33.1 0.7 %copy.9 = f32[9,8,8,128]{3,2,1,0:T(8,128)} copy(f32[9,8,8,128]{3,2,1,0:T(8,128)S(1)} %shard_map.73) | data formatting | bytes 589824

commit v4 on v3

--- a/solution.py
+++ b/solution.py
@@ -276,12 +276,6 @@
             vb[rest, j * 128 : j * 128 + 128] = vf[j, rest, :].astype(BF16)
         return most, rest
 
-    @pl.when(odd == 0)
-    def _():
-        pl.semaphore_wait(ready, len(around))
-        for copy in k_copies:
-            copy.start()
-
     most, rest = unpack(core)
     edges = jnp.concatenate(
         [
@@ -301,8 +295,13 @@
             src_ref=eo.at[n], dst_ref=ezi.at[n, core], send_sem=sendz.at[n, cross], recv_sem=recvz.at[n, cross],
             device_id=(who, other), device_id_type=MESH,
         )
-        copy.start()
         z_copies.append(copy)
+
+    @pl.when(odd == 1)
+    def _():
+        for copy in z_copies:
+            copy.start()
+
     p0, p1 = iota((128, 128), 0), iota((128, 128), 1)
     dz, dy = (p0 // 8) % 8 - (p1 // 8) % 8, p0 % 8 - p1 % 8
     near = (p0 // 64 == p1 // 64) & (dz * dz + dy * dy == 1)
@@ -336,6 +335,12 @@
     low_most, low_rest = shifted_rows(1 - core)
     neighbours(most, low_most)
     neighbours(rest, low_rest)
+
+    @pl.when(odd == 0)
+    def _():
+        pl.semaphore_wait(ready, len(around))
+        for copy in k_copies + z_copies:
+            copy.start()
 
     wbuf[...] = jnp.dot(cc[:, 0:KPAD], vb[:, 0:640], preferred_element_type=F32)
 

time: 33.9 us -> 32.9 us (0.971)
  Pallas kernels: 33.1 us -> 32 us
    pallas_call x1, Pallas kernels: 33.1 us -> 32 us  [body(): call(*(pltpu.with_memory_space_constraint(a, pltpu.HBM) for a in operands))]
where the time goes in v4:
time: 32.9 us; the launch traced here: 32.7 us
  Pallas kernels  32 us (97%)
  local copies, waits for them, and re-layouts  0.72 us (2%)
    pallas_call x1, Pallas kernels, body(): call(*(pltpu.with_memory_space_constraint(a, pltpu.HBM) for a in operands))  32 us
    unnamed x1, local copies, waits for them, and re-layouts  0.72 us

profile of v4, /device:TPU:1, one launch (start us, length us, event | category | flops | bytes accessed | tf_op | source)
XLA Modules:
  0.0 32.7 jit_solution(102584442466315888)
XLA Ops:
  0.0 32.0 %shard_map.73 = f32[9,8,8,128]{3,2,1,0:T(8,128)S(1)} custom-call(bf16[9,8,8,128]{3,2,1,0:T(8,128)(2,1)} %v_hbm.1, f32[11,8,8,128]{3,2,1,0:T(8,128)} %k_hbm.1, s32[286]{0:T(512)} %slot_hbm.1, s32[1606]{0:T(1024)} %kl_hbm.1, s32[1606]{0:T(1024)} %in_hbm.1, s32[1606]{0:T(1024)} %out_hbm.1, bf16[1606]{0:T(1024)(128)(2,1)} %w_hbm.1), custom_call_target="tpu_custom_call" | custom-call | tf_op jit(solution)/shard_map/pallas_call | solution.py:505
  32.0 0.7 %copy.9 = f32[9,8,8,128]{3,2,1,0:T(8,128)} copy(f32[9,8,8,128]{3,2,1,0:T(8,128)S(1)} %shard_map.73) | data formatting | bytes 589824

commit v5 on v4

--- a/solution.py
+++ b/solution.py
@@ -128,6 +128,9 @@
 
     for copy in loads[1:]:
         copy.start()
+
+    for j in range(4, 8):
+        ans[pl.ds(32 + j, CHIPS, stride=ANS), :] = jnp.zeros((CHIPS, 128), F32)
 
     row = iota((256, 128), 0)
     select = column_select(256, (row % 128) // 8, row // 128, row % 8)
@@ -420,8 +423,6 @@
         for c in range(CHIPS):
             ans[c * ANS + j * 8 : c * ANS + j * 8 + 8, :] = total[c * 8 : c * 8 + 8]
         ans[pl.ds(32 + j, CHIPS, stride=ANS), :] = total[128:ROWS]
-    for j in range(4, 8):
-        ans[pl.ds(32 + j, CHIPS, stride=ANS), :] = jnp.zeros((CHIPS, 128), F32)
 
     def block_of(c):
         return pl.ds(pl.multiple_of(c * ANS, 8), ANS)
@@ -439,15 +440,17 @@
     low16 = iota((CHIPS, 128), 1) < 64
     for first in range(0, OWN, 2):
         second = min(first + 1, OWN - 1)
+        base = first * 64
         for j in range(4):
             one = ret[pl.ds(j * 8 + first if first < 8 else 32 + j, CHIPS, stride=ANS), :]
             two = ret[pl.ds(j * 8 + second if second < 8 else 32 + j, CHIPS, stride=ANS), :]
-            turn[pl.ds(j, CHIPS, stride=8), :] = jnp.where(low16, one, pltpu.roll(two, 64, 1))
-            turn[pl.ds(4 + j, CHIPS, stride=8), :] = jnp.where(low16, pltpu.roll(one, 64, 1), two)
-        turned = turn[...].T
+            turn[pl.ds(base + j, CHIPS, stride=8), :] = jnp.where(low16, one, pltpu.roll(two, 64, 1))
+            turn[pl.ds(base + 4 + j, CHIPS, stride=8), :] = jnp.where(low16, pltpu.roll(one, 64, 1), two)
+    for first in range(0, OWN, 2):
+        turned = turn[first * 64 : first * 64 + 128, :].T
         o_ref[first] = turned[:64].reshape(8, 8, 128)
-        if second > first:
-            o_ref[second] = turned[64:].reshape(8, 8, 128)
+        if first + 1 < OWN:
+            o_ref[first + 1] = turned[64:].reshape(8, 8, 128)
 
     sent = msg.at[pl.ds(0, CHIPS - 1)]
     pltpu.make_async_copy(sent, sent, send1).wait()
@@ -492,7 +495,7 @@
             pltpu.VMEM((ROWS, 128), F32),
             pltpu.VMEM((CHIPS * ANS, 128), F32),
             pltpu.VMEM((CHIPS * ANS, 128), F32),
-            pltpu.VMEM((128, 128), F32),
+            pltpu.VMEM((640, 128), F32),
             pltpu.VMEM((16, KPAD), F32),
             pltpu.VMEM((8, TRIPS_PAD), jnp.int32),
             pltpu.VMEM((8, TRIPS_PAD), F32),

time: 32.9 us -> 32.9 us (level)
  no operation moved by 1% of the time
where the time goes in v5:
time: 32.9 us; the launch traced here: 32.7 us
  Pallas kernels  32 us (97%)
  local copies, waits for them, and re-layouts  0.72 us (2%)
    pallas_call x1, Pallas kernels, body(): call(*(pltpu.with_memory_space_constraint(a, pltpu.HBM) for a in operands))  32 us
    unnamed x1, local copies, waits for them, and re-layouts  0.72 us

profile of v5, /device:TPU:1, one launch (start us, length us, event | category | flops | bytes accessed | tf_op | source)
XLA Modules:
  0.0 32.7 jit_solution(6379811092799168386)
XLA Ops:
  0.0 32.0 %shard_map.73 = f32[9,8,8,128]{3,2,1,0:T(8,128)S(1)} custom-call(bf16[9,8,8,128]{3,2,1,0:T(8,128)(2,1)} %v_hbm.1, f32[11,8,8,128]{3,2,1,0:T(8,128)} %k_hbm.1, s32[286]{0:T(512)} %slot_hbm.1, s32[1606]{0:T(1024)} %kl_hbm.1, s32[1606]{0:T(1024)} %in_hbm.1, s32[1606]{0:T(1024)} %out_hbm.1, bf16[1606]{0:T(1024)(128)(2,1)} %w_hbm.1), custom_call_target="tpu_custom_call" | custom-call | tf_op jit(solution)/shard_map/pallas_call | solution.py:508
  32.0 0.7 %copy.9 = f32[9,8,8,128]{3,2,1,0:T(8,128)} copy(f32[9,8,8,128]{3,2,1,0:T(8,128)S(1)} %shard_map.73) | data formatting | bytes 589824

commit v6 on v5

--- a/solution.py
+++ b/solution.py
@@ -152,17 +152,17 @@
 
     pl.semaphore_wait(barrier, len(offsets) + 1 + len(around) * odd)
 
-    @pl.when(odd == 1)
-    def _():
-        for _, who, other in around:
-            pl.semaphore_signal(ready, inc=1, device_id=(who, other), device_id_type=MESH)
-
     for ky, kx in offsets:
         target = chip_at(ky, kx)
         pltpu.make_async_remote_copy(
             src_ref=msg.at[target], dst_ref=got.at[core, ky * SIDE + kx], send_sem=send1, recv_sem=recv1.at[ky],
             device_id=(target * 2 + core, zi), device_id_type=MESH,
         ).start()
+
+    @pl.when(odd == 1)
+    def _():
+        for _, who, other in around:
+            pl.semaphore_signal(ready, inc=1, device_id=(who, other), device_id_type=MESH)
 
     gather_edge = edge_gather()
     spread_edge = edge_spread()
@@ -406,13 +406,12 @@
         vb[256 + half * 16 : 272 + half * 16, 640:768] = two[48:64]
     hbuf[...] = jnp.dot(cc[:, 0:KPAD], vb[:, 640:768], preferred_element_type=F32)
 
-    @pl.loop(0, ROWS // 16)
-    def _(block):
+    for block in range(ROWS // 16):
         ends = jnp.zeros((16, 128), F32)
         for i in range(TERMS):
-            at = pl.ds(pl.multiple_of(i * ROWS + block * 16, 16), 16)
+            at = slice(i * ROWS + block * 16, i * ROWS + block * 16 + 16)
             ends = ends + hzc[i : i + 1, :] * hbuf[at, :]
-        ez[pl.ds(pl.multiple_of(block * 16, 16), 16), :] = ends
+        ez[block * 16 : block * 16 + 16, :] = ends
 
     end_parts = jnp.zeros((ROWS, 512), F32)
     for piece in reversed(split(ez[...], 2)):

time: 32.9 us -> 32.7 us (level)
  no operation moved by 1% of the time
where the time goes in v6:
time: 32.7 us; the launch traced here: 32.6 us
  Pallas kernels  31.8 us (97%)
  local copies, waits for them, and re-layouts  0.72 us (2%)
    pallas_call x1, Pallas kernels, body(): call(*(pltpu.with_memory_space_constraint(a, pltpu.HBM) for a in operands))  31.8 us
    unnamed x1, local copies, waits for them, and re-layouts  0.72 us

profile of v6, /device:TPU:1, one launch (start us, length us, event | category | flops | bytes accessed | tf_op | source)
XLA Modules:
  0.0 32.6 jit_solution(6543133480032148101)
XLA Ops:
  0.0 31.8 %shard_map.73 = f32[9,8,8,128]{3,2,1,0:T(8,128)S(1)} custom-call(bf16[9,8,8,128]{3,2,1,0:T(8,128)(2,1)} %v_hbm.1, f32[11,8,8,128]{3,2,1,0:T(8,128)} %k_hbm.1, s32[286]{0:T(512)} %slot_hbm.1, s32[1606]{0:T(1024)} %kl_hbm.1, s32[1606]{0:T(1024)} %in_hbm.1, s32[1606]{0:T(1024)} %out_hbm.1, bf16[1606]{0:T(1024)(128)(2,1)} %w_hbm.1), custom_call_target="tpu_custom_call" | custom-call | tf_op jit(solution)/shard_map/pallas_call | solution.py:507
  31.8 0.7 %copy.9 = f32[9,8,8,128]{3,2,1,0:T(8,128)} copy(f32[9,8,8,128]{3,2,1,0:T(8,128)S(1)} %shard_map.73) | data formatting | bytes 589824
